TPU v7x, 128 devices: a whole 4x4x4 slice. The times are simulated.
128 devices in a mesh: fib: 32 (over y, x, z_lo), xs: 4 (over z_hi, core).
Axes of the slice: x: 4, y: 4, z: 4 (z_hi: 2, z_lo: 2; z = z_hi * 2 + z_lo), core: 2. Of those that a mesh axis runs over, the one named last changes fastest.
Arguments:
- inverse_blocks: bfloat16 [32, 1536, 128, 128], P('fib', 'xs')
- constraint_rows: bfloat16 [96, 32, 196608], P(None, 'fib', 'xs'), may hold values from -6 to 6
- probe: bfloat16 [8192, 128], P(('fib', 'xs')), may hold values from -6 to 6
- face_offset: int32 [32, 4], P('fib', 'xs'), may hold values from 1 to 3
- primal_ids: int32 [32, 4, 96], P('fib', 'xs'), may hold values from 0 to 8191, as said below
- active_counts: int32 [32, 4], P('fib', 'xs'), may hold values from 48 to 96
Outputs:
- face_basis: bfloat16 [96, 32, 1536], P(None, 'fib', 'xs')
- coarse_apply: float32 [8192, 128], P(('fib', 'xs'))
Inputs may be any that keep to these rules, and one draw needn't show every extreme that they name: `primal_ids`: column j of subdomain s (s = f * 4 + x) belongs to an owner subdomain (s + t) mod 128 with t one of 0, 1, -1, 2, -2, 3, -3 and 64, owner subdomain o owning ids o * 64 to (o + 1) * 64 - 1; at most 16 columns of one subdomain go to one owner, and exactly 16 to some owner in every subdomain.
All inputs are finite; a program needn't handle non-finite values.
Results may differ from a plain program's by a relative error of at most 0.0055.
Values may be sent and summed in bfloat16 or wider, within the bound.
A program may use at most 128 MiB of HBM per device.

v0:
```python
import jax
import jax.numpy as jnp
from jax import lax
from jax.sharding import PartitionSpec as P

NEAR = 8


def extended(cells, sides, width):
    for axis, dim in sides:
        count = lax.axis_size(axis)
        head = lax.slice_in_dim(cells, 0, width, axis=dim)
        tail = lax.slice_in_dim(cells, cells.shape[dim] - width, cells.shape[dim], axis=dim)
        cells = jnp.concatenate(
            [
                lax.ppermute(tail, axis, [(i, (i + 1) % count) for i in range(count)]),
                cells,
                lax.ppermute(head, axis, [((i + 1) % count, i) for i in range(count)]),
            ],
            axis=dim,
        )
    return cells


def owner_shift(k, devices_n):
    if k == 0:
        return 0
    if k == 7:
        return devices_n // 2
    if k % 2 == 1:
        return (k + 1) // 2
    return -(k // 2)


def shards(inverse_blocks, constraint_rows, probe, face_offset, primal_ids, active_counts):
    inverse_local = inverse_blocks[0]
    local_rows = constraint_rows[:, 0, :]
    columns_n, rows_dev = local_rows.shape
    block_count, block_size = (inverse_local.shape[0], inverse_local.shape[1])
    owned_n, vectors_n = probe.shape
    basis = (
        jnp.einsum(
            "nab,jnb->jna",
            inverse_local,
            local_rows.reshape(columns_n, block_count, block_size),
            preferred_element_type=jnp.float32,
        )
        .reshape(columns_n, rows_dev)
        .astype(jnp.bfloat16)
    )
    padded = extended(basis, (("fib", 1),), block_size)
    before_high = padded[:, :block_size].astype(jnp.float32)
    after_low = padded[:, rows_dev + block_size :].astype(jnp.float32)
    low_face = basis[:, :block_size].astype(jnp.float32)
    cross_face = basis[:, block_size : 2 * block_size]
    high_face = basis[:, rows_dev - block_size :].astype(jnp.float32)
    stacked = lax.all_gather(cross_face[None], "xs", axis=0, tiled=True)
    partner = (lax.axis_index("xs") + face_offset[0, 0]) % lax.axis_size("xs")
    partner_face = lax.dynamic_index_in_dim(stacked, partner, 0, keepdims=False).astype(jnp.float32)
    new_low = (0.5 * (low_face + before_high)).astype(jnp.bfloat16)
    new_high = (0.5 * (high_face + after_low)).astype(jnp.bfloat16)
    new_cross = (0.5 * (cross_face.astype(jnp.float32) + partner_face)).astype(jnp.bfloat16)
    face_basis = jnp.concatenate([new_low, new_cross, new_high], axis=1)[:, None, :]
    averaged = jnp.concatenate(
        [new_low, new_cross, basis[:, 2 * block_size : rows_dev - block_size], new_high], axis=1
    )
    coarse = (
        lax.dot_general(
            averaged, local_rows, (((1,), (1,)), ((), ())), preferred_element_type=jnp.float32
        )
        / rows_dev
    )
    positions = jnp.arange(columns_n, dtype=jnp.int32)
    active = (positions < active_counts[0, 0]).astype(jnp.float32)
    coarse = coarse * active[:, None] * active[None, :]
    column_ids = primal_ids[0, 0]
    devices_n = lax.axis_size("fib") * lax.axis_size("xs")
    my_index = lax.axis_index("fib") * lax.axis_size("xs") + lax.axis_index("xs")
    owners = column_ids // owned_n
    shifts = [owner_shift(k, devices_n) for k in range(NEAR)]
    delta = (owners - my_index) % devices_n
    offsets = jnp.zeros_like(delta)
    for k in range(NEAR):
        offsets = offsets + k * (delta == shifts[k] % devices_n).astype(jnp.int32)
    whole_probe = lax.all_gather(probe, ("fib", "xs"), axis=0, tiled=True)
    probe_rows = jnp.take(whole_probe, column_ids, axis=0).astype(jnp.float32)
    partial_value = jnp.dot(coarse, probe_rows, precision=lax.Precision.HIGHEST)
    dense_terms = (
        jnp.zeros((devices_n * owned_n, vectors_n), jnp.float32).at[column_ids].add(partial_value)
    )
    coarse_apply = lax.psum_scatter(dense_terms, ("fib", "xs"), scatter_dimension=0, tiled=True)
    return (face_basis, coarse_apply)


def solution(mesh):
    return jax.shard_map(
        shards,
        mesh=mesh,
        in_specs=(
            P("fib", "xs", None, None),
            P(None, "fib", "xs"),
            P(("fib", "xs"), None),
            P("fib", "xs"),
            P("fib", "xs", None),
            P("fib", "xs"),
        ),
        out_specs=(P(None, "fib", "xs"), P(("fib", "xs"), None)),
        check_vma=False,
    )
```

profile of v0, /device:TPU:1, one launch (start us, length us, event | category | flops | bytes accessed | tf_op | source)
XLA Modules:
  0.0 854.4 jit_solution(8957609233361429159)
XLA Ops:
  7.2 0.0 all-gather.3.cloned.1.call-start
  7.2 0.7 all-gather.3.cloned.1.call-update
  7.9 0.0 reduce-scatter.2.cloned.1.call-start
  7.9 10.0 %copy.12 = bf16[12,8,384,128]{3,2,1,0:T(8,128)(2,1)} copy(bf16[12,8,384,128]{3,1,2,0:T(8,128)(2,1)} %bitcast.44) | data formatting | bytes 18874368
  18.0 27.0 %convert_bitcast_fusion = bf16[384,12,8,128]{3,2,1,0:T(8,128)(2,1)} fusion(bf16[1,384,128,128]{3,2,1,0:T(8,128)(2,1)} %param.6, bf16[96,384,128]{2,1,0:T(8,128)(2,1)} %bitcast.40), kind=kOutput, calls=%fused_computation.15 | convolution fusion | flops 1212678144 | bytes 31457280 | tf_op jit(solution)/shard_map/nab,jnb->jna/dot_general | solution.py:42
  44.9 9.6 %copy.18 = bf16[384,12,8,128]{3,2,0,1:T(8,128)(2,1)} copy(bf16[384,12,8,128]{3,2,1,0:T(8,128)(2,1)} %convert_bitcast_fusion) | data formatting | bytes 18874368 | tf_op jit(solution)/shard_map/convert_element_type | solution.py:49
  54.5 0.0 copy-start
  54.5 0.8 fusion.37
  55.3 2.5 collective-permute-start
  57.8 4.7 collective-permute-start.1
  63.1 7.9 slice.23
  71.7 0.0 copy-done
  71.7 7.8 all-gather
  79.5 0.0 collective-permute-done
  79.5 0.0 collective-permute-done.1
  79.5 0.8 multiply_convert_fusion.1
  80.3 8.6 %fusion.23 = f32[96,96]{1,0:T(8,128)S(1)} fusion(bf16[96,1,49152]{2,0,1:T(8,128)(2,1)} %param.7, bf16[96,128]{1,0:T(8,128)(2,1)S(1)} %get-tuple-element.3, bf16[96,48768]{1,0:T(8,128)(2,1)} %slice.23, bf16[96,128]{1,0:T(8,128)(2,1)S(1)} %get-tuple-element.4, bf16[96,128]{1,0:T(8,128)(2,1)S(1)} %get-tuple-element.2, f32[96]{0:T(128)S(1)} %compare_convert_fusion, ...), kind=kOutput, calls=%fused_computation.19 | convolution fusion | flops 943736832 | bytes 18912000 | tf_op jit(solution)/shard_map/dot_general | solution.py:68
  89.0 118.1 %all-gather.3.cloned.1.call-done = bf16[8192,128]{1,0:T(8,128)(2,1)} async-done(((bf16[64,128]{1,0:T(8,128)(2,1)}), bf16[8192,128]{1,0:T(8,128)(2,1)}) %all-gather.3.cloned.1.call-update) | async-done | bytes 2097168 | tf_op jit(solution)/shard_map/all_gather | solution.py:85
  207.1 2.5 gather_fusion
  209.6 0.2 fusion.30
  209.8 3.1 scatter_custom_fusion
  212.9 0.0 reduce-scatter.2.cloned.1.call-update
  212.9 0.6 maximum_bitcast_fusion
  213.5 634.0 %reduce-scatter.2.cloned.1.call-done = f32[64,128]{1,0:T(8,128)} async-done(((f32[8192,128]{1,0:T(8,128)}), f32[64,128]{1,0:T(8,128)}) %reduce-scatter.2.cloned.1.call-update) | async-done | bytes 32784 | tf_op jit(solution)/shard_map/reduce_scatter | solution.py:91
  (5 shorter events, 0.0 us)
Async XLA Ops:
  7.2 199.9 %all-gather.3.cloned.1.call-start = ((), (), s32[]{:S(2)}) async-start(), calls=%async_computation.1 | async-start | bytes 2113536 | tf_op jit(solution)/shard_map/all_gather | solution.py:85
  7.9 839.7 %reduce-scatter.2.cloned.1.call-start = ((), (), s32[]{:S(2)}) async-start(), calls=%async_computation.2 | async-start | bytes 4227072 | tf_op jit(solution)/shard_map/reduce_scatter | solution.py:91
  54.5 17.2 %copy-start = (s32[1,1,96]{2,1,0:T(1,128)S(1)}, s32[1,1,96]{2,1,0:T(1,128)}, u32[]{:S(2)}) copy-start(s32[1,1,96]{2,1,0:T(1,128)} %param.10) | copy-start | bytes 1156
  55.3 24.2 %collective-permute-start = (bf16[96,128]{1,0:T(8,128)(2,1)S(1)}, bf16[96,128]{1,0:T(8,128)(2,1)S(1)}, u32[]{:S(2)}, u32[]{:S(2)}) collective-permute-start(bf16[96,128]{1,0:T(8,128)(2,1)S(1)} %get-tuple-element.5), channel_id=1, source_target_pairs={{0,4},{4,8},{8,12},{12,16},{16,20},{20,24},{24,28},{28,32},{32,36}... | collective-permute-start | bytes 73736 | tf_op jit(solution)/shard_map/ppermute | solution.py:16
  57.8 21.8 %collective-permute-start.1 = (bf16[96,128]{1,0:T(8,128)(2,1)S(1)}, bf16[96,128]{1,0:T(8,128)(2,1)S(1)}, u32[]{:S(2)}, u32[]{:S(2)}) collective-permute-start(bf16[96,128]{1,0:T(8,128)(2,1)S(1)} %get-tuple-element.7), channel_id=1, source_target_pairs={{4,0},{8,4},{12,8},{16,12},{20,16},{24,20},{28,24},{32,28},{36,32}... | collective-permute-start | bytes 73736 | tf_op jit(solution)/shard_map/ppermute | solution.py:18
Sparse Core Ops, SparseCore 0:
  9.7 197.3 all-gather.2
  213.0 634.4 reduce-scatter.1
where the time goes:
time: 861 us; the launch traced here: 854 us
  waiting for transfers between devices  753 us (87%)
  matrix products  35.8 us (4%)
  local copies, waits for them, and re-layouts  30.7 us (4%)
  between operations  15.4 us (2%)
    reduce_scatter x1, waiting for transfers between devices, shards(): lax.psum_scatter(dense_terms, ('fib', 'xs'), scatter_dimension=0, tiled=T...  634 us
    all_gather x1, waiting for transfers between devices, shards(): whole_probe = lax.all_gather(probe, ('fib', 'xs'), axis=0, tiled=True)  118 us
    dot_general x1, matrix products, shards(): jnp.einsum('nab,jnb->jna', inverse_local, local_rows.reshape(columns_n, b...  27 us
  transfers between devices with their start and end apart: 4, of which 2 were waited for; matrix products, arithmetic and copies ran while one was open for 8% of the time, Pallas kernels for 0%

commit v1 on v0

v1 whole, which is shorter than its diff:
```python
import functools

import jax
import jax.numpy as jnp
from jax import lax
from jax.experimental import pallas as pl
from jax.experimental.pallas import tpu as pltpu
from jax.sharding import PartitionSpec as P

SHIFTS = (0, 1, -1, 2, -2, 3, -3, 64)
NEAR = 8
GREETED = (1, -1, 2, -2, 3, -3, 4, -4, 64)
CHUNK = 20
MESH = pl.DeviceIdType.MESH
NT = (((1,), (1,)), ((), ()))
NN = (((1,), (0,)), ((), ()))
TN = (((0,), (0,)), ((), ()))
BF = jnp.bfloat16
F32 = jnp.float32


def dot(a, b, dims):
    return lax.dot_general(a, b, dims, preferred_element_type=F32)


def kernel(
    n_fib,
    n_xs,
    inv_hbm,
    rows_hbm,
    probe_hbm,
    ids_ref,
    offset_ref,
    count_ref,
    face_out,
    apply_out,
    inv_v,
    rows_v,
    inv_e,
    rows_e,
    own_v,
    fib_v,
    cross_v,
    near_v,
    select_v,
    part_v,
    recv_v,
    local_sem,
    inv_sem,
    rows_sem,
    fib_send,
    fib_recv,
    cross_send,
    cross_recv,
    probe_send,
    probe_recv,
    part_send,
    part_recv,
):
    n_dev = n_fib * n_xs
    chunks = inv_v.shape[0]
    block = inv_v.shape[2]
    blocks = inv_hbm.shape[0]
    primals, rows_dev = rows_hbm.shape
    owned = probe_hbm.shape[0]
    f = lax.axis_index("fib")
    x = lax.axis_index("xs")
    me = f * n_xs + x

    def at(shift):
        index = lax.rem(me + (shift + n_dev), n_dev)
        return (lax.div(index, n_xs), lax.rem(index, n_xs))

    barrier = pltpu.get_barrier_semaphore()
    for shift in GREETED:
        pl.semaphore_signal(barrier, inc=1, device_id=at(shift), device_id_type=MESH)

    ends = [
        pltpu.make_async_copy(inv_hbm.at[pl.ds(0, 2)], inv_e.at[pl.ds(0, 2)], local_sem.at[0]),
        pltpu.make_async_copy(inv_hbm.at[pl.ds(blocks - 2, 2)], inv_e.at[pl.ds(2, 2)], local_sem.at[1]),
        pltpu.make_async_copy(rows_hbm.at[:, pl.ds(0, 2 * block)], rows_e.at[0], local_sem.at[2]),
        pltpu.make_async_copy(
            rows_hbm.at[:, pl.ds(rows_dev - 2 * block, 2 * block)], rows_e.at[1], local_sem.at[3]
        ),
    ]
    own_probe = pltpu.make_async_copy(probe_hbm, near_v.at[pl.ds(0, owned)], local_sem.at[4])
    for copy in ends:
        copy.start()
    own_probe.start()

    def chunk_copies(c):
        width = CHUNK * block
        return (
            pltpu.make_async_copy(inv_hbm.at[pl.ds(2 + c * CHUNK, CHUNK)], inv_v.at[c], inv_sem.at[c]),
            pltpu.make_async_copy(
                rows_hbm.at[:, pl.ds(pl.multiple_of(2 * block + c * width, block), width)],
                rows_v.at[c],
                rows_sem.at[c],
            ),
        )

    def start_chunk(c, carry):
        for copy in chunk_copies(c):
            copy.start()
        return carry

    lax.fori_loop(0, chunks, start_chunk, 0)

    ids = ids_ref[...]
    owner = lax.shift_right_logical(ids, 6)
    delta = owner - me
    delta = jnp.where(delta < 0, delta + n_dev, delta)
    slot = jnp.zeros_like(delta)
    for k in range(1, NEAR):
        slot = jnp.where(delta == (SHIFTS[k] % n_dev), k, slot)
    target = slot * owned + (ids - owner * owned)
    lane = lax.broadcasted_iota(jnp.int32, ids.shape, 1)
    target = jnp.where(lane < count_ref[0, 0], target, -1)
    wanted = lax.broadcasted_iota(jnp.int32, (NEAR * owned, primals), 0)
    select_v[...] = jnp.where(wanted == target, 1.0, 0.0).astype(BF)

    for copy in ends:
        copy.wait()

    def edge(e, h):
        return dot(rows_e[e, :, h * block : (h + 1) * block], inv_e[2 * e + h], NT).astype(BF)

    own_v[0] = edge(0, 0)
    own_v[1] = edge(0, 1)
    own_v[2] = edge(1, 1)
    inner = edge(1, 0)

    pl.semaphore_wait(barrier, len(GREETED))
    before = (lax.rem(f + n_fib - 1, n_fib), x)
    after = (lax.rem(f + 1, n_fib), x)

    def remote(src, dst, send, recv, device):
        return pltpu.make_async_remote_copy(
            src_ref=src, dst_ref=dst, send_sem=send, recv_sem=recv, device_id=device, device_id_type=MESH
        )

    sends = [
        remote(own_v.at[2], fib_v.at[0], fib_send.at[0], fib_recv.at[0], after),
        remote(own_v.at[0], fib_v.at[1], fib_send.at[1], fib_recv.at[1], before),
    ]
    for d in range(1, n_xs):
        to = (f, lax.rem(x + n_xs - d, n_xs))
        sends.append(remote(own_v.at[1], cross_v.at[d - 1], cross_send.at[d - 1], cross_recv.at[d - 1], to))
    for k in range(1, NEAR):
        sends.append(
            remote(
                probe_hbm,
                near_v.at[pl.ds(k * owned, owned)],
                probe_send.at[k - 1],
                probe_recv.at[k - 1],
                at(-SHIFTS[k]),
            )
        )
    for copy in sends:
        copy.start()

    def body(c, acc):
        for copy in chunk_copies(c):
            copy.wait()
        parts = []
        for i in range(CHUNK):
            parts.append(dot(rows_v[c, :, i * block : (i + 1) * block], inv_v[c, i], NT).astype(BF))
        return acc + dot(jnp.concatenate(parts, axis=1), rows_v[c], NT)

    coarse = lax.fori_loop(0, chunks, body, jnp.zeros((primals, primals), F32))

    own_probe.wait()
    for copy in sends:
        copy.wait()
    picked = dot(select_v[...], near_v[...], TN).astype(BF)

    offset = offset_ref[0, 0]
    partner = cross_v[0].astype(F32)
    for d in range(2, n_xs):
        partner = jnp.where(offset == d, cross_v[d - 1].astype(F32), partner)
    new_low = (0.5 * (own_v[0].astype(F32) + fib_v[0].astype(F32))).astype(BF)
    new_high = (0.5 * (own_v[2].astype(F32) + fib_v[1].astype(F32))).astype(BF)
    new_cross = (0.5 * (own_v[1].astype(F32) + partner)).astype(BF)
    face_out[:, 0:block] = new_low
    face_out[:, block : 2 * block] = new_cross
    face_out[:, 2 * block : 3 * block] = new_high
    coarse = coarse + dot(jnp.concatenate([new_low, new_cross], axis=1), rows_e[0], NT)
    coarse = coarse + dot(jnp.concatenate([inner, new_high], axis=1), rows_e[1], NT)
    coarse = coarse * (1.0 / rows_dev)

    def pieces(value):
        high = value.astype(BF)
        low = (value - high.astype(F32)).astype(BF)
        return high, low

    c_high, c_low = pieces(coarse)
    partial = dot(c_high, picked, NN) + dot(c_low, picked, NN)
    p_high, p_low = pieces(partial)
    dense = dot(select_v[...], p_high, NN) + dot(select_v[...], p_low, NN)
    part_v[...] = dense

    outs = []
    for k in range(1, NEAR):
        outs.append(
            remote(
                part_v.at[pl.ds(k * owned, owned)],
                recv_v.at[k - 1],
                part_send.at[k - 1],
                part_recv.at[k - 1],
                at(SHIFTS[k]),
            )
        )
    for copy in outs:
        copy.start()
    for copy in outs:
        copy.wait()
    total = part_v[0:owned, :]
    for k in range(1, NEAR):
        total = total + recv_v[k - 1]
    apply_out[...] = total


def shards(n_fib, n_xs, inverse_blocks, constraint_rows, probe, face_offset, primal_ids, active_counts):
    inv = inverse_blocks[0]
    rows = constraint_rows[:, 0, :]
    blocks, block, _ = inv.shape
    primals, rows_dev = rows.shape
    owned, vectors = probe.shape
    chunks = (blocks - 4) // CHUNK
    dma = pltpu.SemaphoreType.DMA
    faces, applied = pl.pallas_call(
        functools.partial(kernel, n_fib, n_xs),
        out_shape=(
            jax.ShapeDtypeStruct((primals, 3 * block), BF),
            jax.ShapeDtypeStruct((owned, vectors), F32),
        ),
        in_specs=[
            pl.BlockSpec(memory_space=pl.ANY),
            pl.BlockSpec(memory_space=pl.ANY),
            pl.BlockSpec(memory_space=pl.ANY),
            pl.BlockSpec(memory_space=pltpu.VMEM),
            pl.BlockSpec(memory_space=pltpu.SMEM),
            pl.BlockSpec(memory_space=pltpu.SMEM),
        ],
        out_specs=(
            pl.BlockSpec(memory_space=pltpu.VMEM),
            pl.BlockSpec(memory_space=pltpu.VMEM),
        ),
        scratch_shapes=[
            pltpu.VMEM((chunks, CHUNK, block, block), BF),
            pltpu.VMEM((chunks, primals, CHUNK * block), BF),
            pltpu.VMEM((4, block, block), BF),
            pltpu.VMEM((2, primals, 2 * block), BF),
            pltpu.VMEM((3, primals, block), BF),
            pltpu.VMEM((2, primals, block), BF),
            pltpu.VMEM((n_xs - 1, primals, block), BF),
            pltpu.VMEM((NEAR * owned, vectors), BF),
            pltpu.VMEM((NEAR * owned, primals), BF),
            pltpu.VMEM((NEAR * owned, vectors), F32),
            pltpu.VMEM((NEAR - 1, owned, vectors), F32),
            dma((5,)),
            dma((chunks,)),
            dma((chunks,)),
            dma((2,)),
            dma((2,)),
            dma((n_xs - 1,)),
            dma((n_xs - 1,)),
            dma((NEAR - 1,)),
            dma((NEAR - 1,)),
            dma((NEAR - 1,)),
            dma((NEAR - 1,)),
        ],
        compiler_params=pltpu.CompilerParams(
            collective_id=0, has_side_effects=True, vmem_limit_bytes=48 * 1024 * 1024
        ),
        name="coarse_setup",
    )(inv, rows, probe, primal_ids[0], face_offset, active_counts)
    return faces[:, None, :], applied


def solution(mesh):
    return jax.shard_map(
        functools.partial(shards, mesh.shape["fib"], mesh.shape["xs"]),
        mesh=mesh,
        in_specs=(
            P("fib", "xs", None, None),
            P(None, "fib", "xs"),
            P(("fib", "xs"), None),
            P("fib", "xs"),
            P("fib", "xs", None),
            P("fib", "xs"),
        ),
        out_specs=(P(None, "fib", "xs"), P(("fib", "xs"), None)),
        check_vma=False,
    )
```

time: 861 us -> 34.4 us (0.04)
  waiting for transfers between devices: 753 us -> 0 us
  matrix products: 35.8 us -> 0 us
  Pallas kernels: 0 us -> 29.6 us
  local copies, waits for them, and re-layouts: 30.7 us -> 2.61 us
  between operations: 15.4 us -> 1.94 us
    reduce_scatter x1 -> x0, waiting for transfers between devices: 634 us -> none  [shards(): lax.psum_scatter(dense_terms, ('fib', 'xs'), scatter_dimension=0, tiled=T...]
    all_gather x1 -> x0, waiting for transfers between devices: 118 us -> none  [shards(): whole_probe = lax.all_gather(probe, ('fib', 'xs'), axis=0, tiled=True)]
    dot_general x3 -> x0, matrix products: 35.8 us -> none  [the longest x1 27 us: shards(): jnp.einsum('nab,jnb->jna', inverse_local, local_rows.reshape(columns_n, b...]
    pallas_call x0 -> x1, Pallas kernels: none -> 29.6 us  [shards(): pl.pallas_call(functools.partial(kernel, n_fib, n_xs), out_shape=(jax.Sha...]
    convert_element_type x1 -> x0, local copies, waits for them, and re-layouts: 9.56 us -> none  [shards(): basis = jnp.einsum('nab,jnb->jna', inverse_local, local_rows.reshape(colu...]
    slice x2 -> x0, local copies, waits for them, and re-layouts: 8.66 us -> none  [the longest x1 7.88 us: shards(): basis[:, 2 * block_size:rows_dev - block_size]]
  transfers between devices with their start and end apart: 4 -> 0, of which waited for: 2 -> 0; matrix products, arithmetic and copies ran while one was open for 8% -> 0% of each run, Pallas kernels for 0% -> 0%
where the time goes in v1:
time: 34.4 us; the launch traced here: 34.2 us
  Pallas kernels  29.6 us (86%)
  local copies, waits for them, and re-layouts  2.61 us (8%)
  between operations  1.94 us (6%)
    pallas_call x1, Pallas kernels, shards(): pl.pallas_call(functools.partial(kernel, n_fib, n_xs), out_shape=(jax.Sha...  29.6 us
    unnamed x6, local copies, waits for them, and re-layouts  2.61 us

profile of v1, /device:TPU:1, one launch (start us, length us, event | category | flops | bytes accessed | tf_op | source)
XLA Modules:
  0.0 34.2 jit_solution(18268929001882900517)
XLA Ops:
  1.9 0.0 copy-start
  1.9 0.7 %copy-done = bf16[64,128]{1,0:T(8,128)(2,1)S(1)} copy-done((bf16[64,128]{1,0:T(8,128)(2,1)S(1)}, bf16[64,128]{1,0:T(8,128)(2,1)}, u32[]{:S(2)}) %copy-start) | copy-done | bytes 16408
  2.6 0.0 copy-start.1
  2.6 0.7 %copy-done.1 = s32[1,1,96]{2,1,0:T(1,128)S(1)} copy-done((s32[1,1,96]{2,1,0:T(1,128)S(1)}, s32[1,1,96]{2,1,0:T(1,128)}, u32[]{:S(2)}) %copy-start.1) | copy-done | bytes 408
  3.3 29.6 %coarse_setup.1 = (bf16[96,384]{1,0:T(8,128)(2,1)S(1)}, f32[64,128]{1,0:T(8,128)S(1)}) custom-call(bf16[384,128,128]{2,1,0:T(8,128)(2,1)} %bitcast.6, bf16[96,49152]{1,0:T(8,128)(2,1)} %bitcast.7, bf16[64,128]{1,0:T(8,128)(2,1)S(1)} %copy-done, s32[1,96]{1,0:T(1,128)S(1)} %bitcast.5, s32[1,1]{1,0:T(1,128)S(6)} %copy.10.offset_ref, s32[1,1]{1,0:T(1,128)S(6)} %copy.11.count_ref), custom_call_target="tpu_custom_call" | custom-call | tf_op jit(solution)/shard_map/coarse_setup/pallas_call | solution.py:231
  32.9 0.6 %copy.12 = bf16[96,1,384]{2,0,1:T(8,128)(2,1)} copy(bf16[96,1,384]{2,0,1:T(8,128)(2,1)S(1)} %bitcast.4) | data formatting | bytes 147456
  33.6 0.6 %copy.13 = f32[64,128]{1,0:T(8,128)} copy(f32[64,128]{1,0:T(8,128)S(1)} %get-tuple-element.9) | data formatting | bytes 65536
Async XLA Ops:
  1.9 0.7 %copy-start = (bf16[64,128]{1,0:T(8,128)(2,1)S(1)}, bf16[64,128]{1,0:T(8,128)(2,1)}, u32[]{:S(2)}) copy-start(bf16[64,128]{1,0:T(8,128)(2,1)} %probe_hbm.1) | copy-start | bytes 49156
  2.6 0.7 %copy-start.1 = (s32[1,1,96]{2,1,0:T(1,128)S(1)}, s32[1,1,96]{2,1,0:T(1,128)}, u32[]{:S(2)}) copy-start(s32[1,1,96]{2,1,0:T(1,128)} %param.10) | copy-start | bytes 1156

commit v2 on v1

--- a/solution.py
+++ b/solution.py
@@ -10,7 +10,10 @@
 SHIFTS = (0, 1, -1, 2, -2, 3, -3, 64)
 NEAR = 8
 GREETED = (1, -1, 2, -2, 3, -3, 4, -4, 64)
-CHUNK = 20
+CHUNK = 38
+CAP = 16
+MIDDLE = 1
+DEPTH = 4
 MESH = pl.DeviceIdType.MESH
 NT = (((1,), (1,)), ((), ()))
 NN = (((1,), (0,)), ((), ()))
@@ -29,13 +32,15 @@
     inv_hbm,
     rows_hbm,
     probe_hbm,
-    ids_ref,
-    offset_ref,
-    count_ref,
+    ids_hbm,
+    offset_hbm,
+    count_hbm,
     face_out,
     apply_out,
     inv_v,
     rows_v,
+    turned_a,
+    turned_b,
     inv_e,
     rows_e,
     own_v,
@@ -43,8 +48,14 @@
     cross_v,
     near_v,
     select_v,
+    pack_v,
+    where_v,
+    places_v,
     part_v,
     recv_v,
+    ids_v,
+    offset_s,
+    count_s,
     local_sem,
     inv_sem,
     rows_sem,
@@ -54,6 +65,8 @@
     cross_recv,
     probe_send,
     probe_recv,
+    place_send,
+    place_recv,
     part_send,
     part_recv,
 ):
@@ -83,41 +96,56 @@
             rows_hbm.at[:, pl.ds(rows_dev - 2 * block, 2 * block)], rows_e.at[1], local_sem.at[3]
         ),
     ]
-    own_probe = pltpu.make_async_copy(probe_hbm, near_v.at[pl.ds(0, owned)], local_sem.at[4])
-    for copy in ends:
+    small = [
+        pltpu.make_async_copy(ids_hbm, ids_v, local_sem.at[4]),
+        pltpu.make_async_copy(offset_hbm, offset_s, local_sem.at[5]),
+        pltpu.make_async_copy(count_hbm, count_s, local_sem.at[6]),
+    ]
+    own_probe = pltpu.make_async_copy(probe_hbm, near_v.at[pl.ds(0, owned)], local_sem.at[7])
+    for copy in ends + small + [own_probe]:
         copy.start()
-    own_probe.start()
-
-    def chunk_copies(c):
-        width = CHUNK * block
-        return (
-            pltpu.make_async_copy(inv_hbm.at[pl.ds(2 + c * CHUNK, CHUNK)], inv_v.at[c], inv_sem.at[c]),
-            pltpu.make_async_copy(
-                rows_hbm.at[:, pl.ds(pl.multiple_of(2 * block + c * width, block), width)],
-                rows_v.at[c],
-                rows_sem.at[c],
-            ),
-        )
+
+    width = CHUNK * block
+
+    def inv_copy(c):
+        return pltpu.make_async_copy(inv_hbm.at[pl.ds(2 + c * CHUNK, CHUNK)], inv_v.at[c], inv_sem.at[c])
+
+    def rows_copy(c):
+        start = pl.multiple_of(2 * block + c * width, block)
+        return pltpu.make_async_copy(rows_hbm.at[:, pl.ds(start, width)], rows_v.at[c], rows_sem.at[c])
 
     def start_chunk(c, carry):
-        for copy in chunk_copies(c):
-            copy.start()
+        rows_copy(c).start()
+        inv_copy(c).start()
         return carry
 
-    lax.fori_loop(0, chunks, start_chunk, 0)
-
-    ids = ids_ref[...]
+    lax.fori_loop(0, DEPTH, start_chunk, 0)
+
+    for copy in small:
+        copy.wait()
+    ids = ids_v[...]
     owner = lax.shift_right_logical(ids, 6)
     delta = owner - me
     delta = jnp.where(delta < 0, delta + n_dev, delta)
     slot = jnp.zeros_like(delta)
     for k in range(1, NEAR):
         slot = jnp.where(delta == (SHIFTS[k] % n_dev), k, slot)
-    target = slot * owned + (ids - owner * owned)
-    lane = lax.broadcasted_iota(jnp.int32, ids.shape, 1)
-    target = jnp.where(lane < count_ref[0, 0], target, -1)
+    within = ids - owner * owned
+    active = lax.broadcasted_iota(jnp.int32, ids.shape, 1) < count_s[0, 0]
+    slot = jnp.where(active, slot, -1)
     wanted = lax.broadcasted_iota(jnp.int32, (NEAR * owned, primals), 0)
-    select_v[...] = jnp.where(wanted == target, 1.0, 0.0).astype(BF)
+    select_v[...] = jnp.where(wanted == jnp.where(active, slot * owned + within, -1), 1.0, 0.0).astype(BF)
+    member = lax.broadcasted_iota(jnp.int32, (2 * NEAR, primals), 0) == slot
+    ahead = lax.broadcasted_iota(jnp.int32, (primals, primals), 0) < lax.broadcasted_iota(
+        jnp.int32, (primals, primals), 1
+    )
+    counts = dot(jnp.where(member, 1.0, 0.0).astype(BF), jnp.where(ahead, 1.0, 0.0).astype(BF), NN)
+    rank = jnp.sum(jnp.where(member, counts, 0.0), axis=0, keepdims=True).astype(jnp.int32)
+    place = jnp.where(active, slot * CAP + rank, -1)
+    pack = jnp.where(lax.broadcasted_iota(jnp.int32, (NEAR * CAP, primals), 0) == place, 1.0, 0.0).astype(BF)
+    pack_v[...] = pack
+    within_rows = jnp.broadcast_to(within.astype(F32), (2 * NEAR, primals)).astype(BF)
+    where_v[...] = dot(within_rows, pack, NT).astype(BF)
 
     for copy in ends:
         copy.wait()
@@ -130,7 +158,6 @@
     own_v[2] = edge(1, 1)
     inner = edge(1, 0)
 
-    pl.semaphore_wait(barrier, len(GREETED))
     before = (lax.rem(f + n_fib - 1, n_fib), x)
     after = (lax.rem(f + 1, n_fib), x)
 
@@ -156,25 +183,56 @@
                 at(-SHIFTS[k]),
             )
         )
+        sends.append(
+            remote(where_v, places_v.at[k - 1], place_send.at[k - 1], place_recv.at[k - 1], at(SHIFTS[k]))
+        )
+
+    def turn(c, turned):
+        for i in range(CHUNK):
+            turned[i] = rows_v[c, :, i * block : (i + 1) * block].T
+
+    def step(c, turned, acc):
+        parts = [dot(inv_v[c, i], turned[i], NN).astype(BF) for i in range(CHUNK)]
+        return acc + dot(rows_v[c], jnp.concatenate(parts, axis=0), NN)
+
+    def body(p, acc):
+        @pl.when(p == MIDDLE)
+        def _():
+            pl.semaphore_wait(barrier, len(GREETED))
+            for copy in sends:
+                copy.start()
+
+        c = 2 * p
+
+        @pl.when(c + DEPTH < chunks)
+        def _():
+            start_chunk(c + DEPTH, 0)
+            start_chunk(c + DEPTH + 1, 0)
+
+        rows_copy(c + 1).wait()
+        inv_copy(c).wait()
+        turn(c + 1, turned_b)
+        acc = step(c, turned_a, acc)
+        rows_copy(c + 2).wait()
+        inv_copy(c + 1).wait()
+        turn(c + 2, turned_a)
+        return step(c + 1, turned_b, acc)
+
+    rows_copy(0).wait()
+    turn(0, turned_a)
+    coarse = lax.fori_loop(0, chunks // 2 - 1, body, jnp.zeros((primals, primals), F32))
+
+    rows_copy(chunks - 1).wait()
+    inv_copy(chunks - 2).wait()
+    inv_copy(chunks - 1).wait()
+    turn(chunks - 1, turned_b)
+    coarse = step(chunks - 2, turned_a, coarse)
+    coarse = step(chunks - 1, turned_b, coarse)
     for copy in sends:
-        copy.start()
-
-    def body(c, acc):
-        for copy in chunk_copies(c):
-            copy.wait()
-        parts = []
-        for i in range(CHUNK):
-            parts.append(dot(rows_v[c, :, i * block : (i + 1) * block], inv_v[c, i], NT).astype(BF))
-        return acc + dot(jnp.concatenate(parts, axis=1), rows_v[c], NT)
-
-    coarse = lax.fori_loop(0, chunks, body, jnp.zeros((primals, primals), F32))
-
+        copy.wait_recv()
     own_probe.wait()
-    for copy in sends:
-        copy.wait()
-    picked = dot(select_v[...], near_v[...], TN).astype(BF)
-
-    offset = offset_ref[0, 0]
+
+    offset = offset_s[0, 0]
     partner = cross_v[0].astype(F32)
     for d in range(2, n_xs):
         partner = jnp.where(offset == d, cross_v[d - 1].astype(F32), partner)
@@ -184,8 +242,16 @@
     face_out[:, 0:block] = new_low
     face_out[:, block : 2 * block] = new_cross
     face_out[:, 2 * block : 3 * block] = new_high
-    coarse = coarse + dot(jnp.concatenate([new_low, new_cross], axis=1), rows_e[0], NT)
-    coarse = coarse + dot(jnp.concatenate([inner, new_high], axis=1), rows_e[1], NT)
+    coarse = coarse + dot(rows_e[0], jnp.concatenate([new_low, new_cross], axis=1), NT)
+    coarse = coarse + dot(rows_e[1], jnp.concatenate([inner, new_high], axis=1), NT)
+    picked = dot(near_v[...], select_v[...], TN).astype(BF)
+    group = lax.broadcasted_iota(jnp.int32, (1, NEAR * CAP), 1) // CAP
+    places = where_v[0:1, :].astype(F32)
+    for k in range(1, NEAR):
+        places = jnp.where(group == k, places_v[k - 1, 0:1, :].astype(F32), places)
+    spread = lax.broadcasted_iota(jnp.int32, (owned, NEAR * CAP), 0) == places.astype(jnp.int32)
+    spread = jnp.where(spread, 1.0, 0.0).astype(BF)
+
     coarse = coarse * (1.0 / rows_dev)
 
     def pieces(value):
@@ -194,30 +260,31 @@
         return high, low
 
     c_high, c_low = pieces(coarse)
-    partial = dot(c_high, picked, NN) + dot(c_low, picked, NN)
+    partial = dot(picked, c_high, NN) + dot(picked, c_low, NN)
     p_high, p_low = pieces(partial)
-    dense = dot(select_v[...], p_high, NN) + dot(select_v[...], p_low, NN)
-    part_v[...] = dense
 
     outs = []
-    for k in range(1, NEAR):
-        outs.append(
-            remote(
-                part_v.at[pl.ds(k * owned, owned)],
-                recv_v.at[k - 1],
-                part_send.at[k - 1],
-                part_recv.at[k - 1],
-                at(SHIFTS[k]),
-            )
-        )
+    for k in (7, 5, 6, 3, 4, 1, 2):
+        rows_k = pl.ds(k * CAP, CAP)
+        outs.append(remote(part_v.at[rows_k], recv_v.at[rows_k], part_send.at[k - 1], part_recv.at[k - 1], at(SHIFTS[k])))
+    packed = dot(pack_v[...], p_high, NT) + dot(pack_v[...], p_low, NT)
+    part_v[...] = packed
     for copy in outs:
         copy.start()
+    recv_v[0:CAP] = packed[0:CAP]
+    for copy in sends:
+        copy.wait_send()
     for copy in outs:
-        copy.wait()
-    total = part_v[0:owned, :]
-    for k in range(1, NEAR):
-        total = total + recv_v[k - 1]
-    apply_out[...] = total
+        copy.wait_recv()
+    r_high, r_low = pieces(recv_v[...])
+    apply_out[...] = dot(spread, r_high, NN) + dot(spread, r_low, NN)
+    for copy in outs:
+        copy.wait_send()
+
+
+def settle(faces_in, applied_in, faces_out, applied_out):
+    faces_out[...] = faces_in[...]
+    applied_out[...] = applied_in[...]
 
 
 def shards(n_fib, n_xs, inverse_blocks, constraint_rows, probe, face_offset, primal_ids, active_counts):
@@ -238,9 +305,9 @@
             pl.BlockSpec(memory_space=pl.ANY),
             pl.BlockSpec(memory_space=pl.ANY),
             pl.BlockSpec(memory_space=pl.ANY),
-            pl.BlockSpec(memory_space=pltpu.VMEM),
-            pl.BlockSpec(memory_space=pltpu.SMEM),
-            pl.BlockSpec(memory_space=pltpu.SMEM),
+            pl.BlockSpec(memory_space=pl.ANY),
+            pl.BlockSpec(memory_space=pl.ANY),
+            pl.BlockSpec(memory_space=pl.ANY),
         ],
         out_specs=(
             pl.BlockSpec(memory_space=pltpu.VMEM),
@@ -249,6 +316,8 @@
         scratch_shapes=[
             pltpu.VMEM((chunks, CHUNK, block, block), BF),
             pltpu.VMEM((chunks, primals, CHUNK * block), BF),
+            pltpu.VMEM((CHUNK, block, primals), BF),
+            pltpu.VMEM((CHUNK, block, primals), BF),
             pltpu.VMEM((4, block, block), BF),
             pltpu.VMEM((2, primals, 2 * block), BF),
             pltpu.VMEM((3, primals, block), BF),
@@ -256,9 +325,15 @@
             pltpu.VMEM((n_xs - 1, primals, block), BF),
             pltpu.VMEM((NEAR * owned, vectors), BF),
             pltpu.VMEM((NEAR * owned, primals), BF),
-            pltpu.VMEM((NEAR * owned, vectors), F32),
-            pltpu.VMEM((NEAR - 1, owned, vectors), F32),
-            dma((5,)),
+            pltpu.VMEM((NEAR * CAP, primals), BF),
+            pltpu.VMEM((2 * NEAR, NEAR * CAP), BF),
+            pltpu.VMEM((NEAR - 1, 2 * NEAR, NEAR * CAP), BF),
+            pltpu.VMEM((NEAR * CAP, vectors), F32),
+            pltpu.VMEM((NEAR * CAP, vectors), F32),
+            pltpu.VMEM((1, primals), jnp.int32),
+            pltpu.SMEM((1, 1), jnp.int32),
+            pltpu.SMEM((1, 1), jnp.int32),
+            dma((8,)),
             dma((chunks,)),
             dma((chunks,)),
             dma((2,)),
@@ -269,12 +344,24 @@
             dma((NEAR - 1,)),
             dma((NEAR - 1,)),
             dma((NEAR - 1,)),
+            dma((NEAR - 1,)),
+            dma((NEAR - 1,)),
         ],
         compiler_params=pltpu.CompilerParams(
-            collective_id=0, has_side_effects=True, vmem_limit_bytes=48 * 1024 * 1024
+            collective_id=0, has_side_effects=True, vmem_limit_bytes=54 * 1024 * 1024
         ),
         name="coarse_setup",
     )(inv, rows, probe, primal_ids[0], face_offset, active_counts)
+    faces, applied = pl.pallas_call(
+        settle,
+        out_shape=(
+            jax.ShapeDtypeStruct((primals, 3 * block), BF),
+            jax.ShapeDtypeStruct((owned, vectors), F32),
+        ),
+        in_specs=[pl.BlockSpec(memory_space=pltpu.VMEM)] * 2,
+        out_specs=(pl.BlockSpec(memory_space=pltpu.VMEM), pl.BlockSpec(memory_space=pltpu.VMEM)),
+        name="settle",
+    )(faces, applied)
     return faces[:, None, :], applied
 
 

time: 34.4 us -> 27 us (0.78)
  Pallas kernels: 29.6 us -> 24.9 us
  local copies, waits for them, and re-layouts: 2.61 us -> 0 us
    pallas_call x1, Pallas kernels: 29.6 us -> 23.3 us  [shards(): pl.pallas_call(functools.partial(kernel, n_fib, n_xs), out_shape=(jax.Sha...]
    unnamed x6 -> x0, local copies, waits for them, and re-layouts: 2.61 us -> none
    pallas_call x0 -> x1, Pallas kernels: none -> 1.53 us  [shards(): pl.pallas_call(settle, out_shape=(jax.ShapeDtypeStruct((primals, 3 * bloc...]
where the time goes in v2:
time: 27 us; the launch traced here: 26.8 us
  Pallas kernels  24.9 us (92%)
  between operations  1.93 us (7%)
    pallas_call x1, Pallas kernels, shards(): pl.pallas_call(functools.partial(kernel, n_fib, n_xs), out_shape=(jax.Sha...  23.3 us
    pallas_call x1, Pallas kernels, shards(): pl.pallas_call(settle, out_shape=(jax.ShapeDtypeStruct((primals, 3 * bloc...  1.53 us

profile of v2, /device:TPU:1, one launch (start us, length us, event | category | flops | bytes accessed | tf_op | source)
XLA Modules:
  0.0 26.8 jit_solution(9164515690598763063)
XLA Ops:
  1.9 23.3 %coarse_setup.1 = (bf16[96,384]{1,0:T(8,128)(2,1)}, f32[64,128]{1,0:T(8,128)}) custom-call(bf16[384,128,128]{2,1,0:T(8,128)(2,1)} %bitcast.4, bf16[96,49152]{1,0:T(8,128)(2,1)} %bitcast.5, bf16[64,128]{1,0:T(8,128)(2,1)} %probe_hbm.1, s32[1,96]{1,0:T(1,128)} %bitcast.6, s32[1,1]{1,0:T(1,128)S(6)} %copy.8.offset_hbm, s32[1,1]{1,0:T(1,128)S(6)} %copy.9.count_hbm), custom_call_target="tpu_custom_call" | custom-call | tf_op jit(solution)/shard_map/coarse_setup/pallas_call | solution.py:298
  25.3 1.5 %settle.1 = (bf16[96,384]{1,0:T(8,128)(2,1)}, f32[64,128]{1,0:T(8,128)}) custom-call(bf16[96,384]{1,0:T(8,128)(2,1)} %get-tuple-element.6.faces_in, f32[64,128]{1,0:T(8,128)} %get-tuple-element.7.applied_in), custom_call_target="tpu_custom_call" | custom-call | tf_op jit(solution)/shard_map/settle/pallas_call | solution.py:355

commit v3 on v2

--- a/solution.py
+++ b/solution.py
@@ -102,7 +102,7 @@
         pltpu.make_async_copy(count_hbm, count_s, local_sem.at[6]),
     ]
     own_probe = pltpu.make_async_copy(probe_hbm, near_v.at[pl.ds(0, owned)], local_sem.at[7])
-    for copy in ends + small + [own_probe]:
+    for copy in small + ends:
         copy.start()
 
     width = CHUNK * block
@@ -120,9 +120,11 @@
         return carry
 
     lax.fori_loop(0, DEPTH, start_chunk, 0)
-
-    for copy in small:
+    own_probe.start()
+
+    for copy in small + ends:
         copy.wait()
+    rows_copy(0).wait()
     ids = ids_v[...]
     owner = lax.shift_right_logical(ids, 6)
     delta = owner - me
@@ -147,12 +149,14 @@
     within_rows = jnp.broadcast_to(within.astype(F32), (2 * NEAR, primals)).astype(BF)
     where_v[...] = dot(within_rows, pack, NT).astype(BF)
 
-    for copy in ends:
-        copy.wait()
-
     def edge(e, h):
         return dot(rows_e[e, :, h * block : (h + 1) * block], inv_e[2 * e + h], NT).astype(BF)
 
+    def turn(c, turned):
+        for i in range(CHUNK):
+            turned[i] = rows_v[c, :, i * block : (i + 1) * block].T
+
+    turn(0, turned_a)
     own_v[0] = edge(0, 0)
     own_v[1] = edge(0, 1)
     own_v[2] = edge(1, 1)
@@ -187,10 +191,6 @@
             remote(where_v, places_v.at[k - 1], place_send.at[k - 1], place_recv.at[k - 1], at(SHIFTS[k]))
         )
 
-    def turn(c, turned):
-        for i in range(CHUNK):
-            turned[i] = rows_v[c, :, i * block : (i + 1) * block].T
-
     def step(c, turned, acc):
         parts = [dot(inv_v[c, i], turned[i], NN).astype(BF) for i in range(CHUNK)]
         return acc + dot(rows_v[c], jnp.concatenate(parts, axis=0), NN)
@@ -218,8 +218,6 @@
         turn(c + 2, turned_a)
         return step(c + 1, turned_b, acc)
 
-    rows_copy(0).wait()
-    turn(0, turned_a)
     coarse = lax.fori_loop(0, chunks // 2 - 1, body, jnp.zeros((primals, primals), F32))
 
     rows_copy(chunks - 1).wait()
@@ -280,11 +278,6 @@
     apply_out[...] = dot(spread, r_high, NN) + dot(spread, r_low, NN)
     for copy in outs:
         copy.wait_send()
-
-
-def settle(faces_in, applied_in, faces_out, applied_out):
-    faces_out[...] = faces_in[...]
-    applied_out[...] = applied_in[...]
 
 
 def shards(n_fib, n_xs, inverse_blocks, constraint_rows, probe, face_offset, primal_ids, active_counts):
@@ -348,20 +341,10 @@
             dma((NEAR - 1,)),
         ],
         compiler_params=pltpu.CompilerParams(
-            collective_id=0, has_side_effects=True, vmem_limit_bytes=54 * 1024 * 1024
+            collective_id=0, has_side_effects=True, vmem_limit_bytes=46 * 1024 * 1024
         ),
         name="coarse_setup",
-    )(inv, rows, probe, primal_ids[0], face_offset, active_counts)
-    faces, applied = pl.pallas_call(
-        settle,
-        out_shape=(
-            jax.ShapeDtypeStruct((primals, 3 * block), BF),
-            jax.ShapeDtypeStruct((owned, vectors), F32),
-        ),
-        in_specs=[pl.BlockSpec(memory_space=pltpu.VMEM)] * 2,
-        out_specs=(pl.BlockSpec(memory_space=pltpu.VMEM), pl.BlockSpec(memory_space=pltpu.VMEM)),
-        name="settle",
-    )(faces, applied)
+    )(*(pltpu.with_memory_space_constraint(a, pltpu.HBM) for a in (inv, rows, probe, primal_ids[0])), face_offset, active_counts)
     return faces[:, None, :], applied
 
 

time: 27 us -> 26 us (0.963)
  Pallas kernels: 24.9 us -> 22.7 us
  local copies, waits for them, and re-layouts: 0 us -> 1.25 us
    pallas_call x1 -> x0, Pallas kernels: 1.53 us -> none  [shards(): pl.pallas_call(settle, out_shape=(jax.ShapeDtypeStruct((primals, 3 * bloc...]
    unnamed x0 -> x2, local copies, waits for them, and re-layouts: none -> 1.25 us
    pallas_call x1, Pallas kernels: 23.3 us -> 22.7 us  [shards(): pl.pallas_call(functools.partial(kernel, n_fib, n_xs), out_shape=(jax.Sha...]
where the time goes in v3:
time: 26 us; the launch traced here: 25.8 us
  Pallas kernels  22.7 us (87%)
  between operations  1.93 us (7%)
  local copies, waits for them, and re-layouts  1.25 us (5%)
    pallas_call x1, Pallas kernels, shards(): pl.pallas_call(functools.partial(kernel, n_fib, n_xs), out_shape=(jax.Sha...  22.7 us
    unnamed x2, local copies, waits for them, and re-layouts  1.25 us

profile of v3, /device:TPU:1, one launch (start us, length us, event | category | flops | bytes accessed | tf_op | source)
XLA Modules:
  0.0 25.8 jit_solution(1445895751558204776)
XLA Ops:
  1.9 22.7 %coarse_setup.1 = (bf16[96,384]{1,0:T(8,128)(2,1)S(1)}, f32[64,128]{1,0:T(8,128)S(1)}) custom-call(bf16[384,128,128]{2,1,0:T(8,128)(2,1)} %bitcast.5, bf16[96,49152]{1,0:T(8,128)(2,1)} %bitcast.6, bf16[64,128]{1,0:T(8,128)(2,1)} %probe_hbm.1, s32[1,96]{1,0:T(1,128)} %bitcast.7, s32[1,1]{1,0:T(1,128)S(6)} %copy.10.offset_hbm, s32[1,1]{1,0:T(1,128)S(6)} %copy.11.count_hbm), custom_call_target="tpu_custom_call" | custom-call | tf_op jit(solution)/shard_map/coarse_setup/pallas_call | solution.py:291
  24.6 0.6 %copy.12 = bf16[96,1,384]{2,0,1:T(8,128)(2,1)} copy(bf16[96,1,384]{2,0,1:T(8,128)(2,1)S(1)} %bitcast.4) | data formatting | bytes 147456
  25.2 0.6 %copy.13 = f32[64,128]{1,0:T(8,128)} copy(f32[64,128]{1,0:T(8,128)S(1)} %get-tuple-element.9) | data formatting | bytes 65536
